TPU v7x, 256 devices: a whole 4x4x8 slice. The times are simulated.
256 devices in a mesh: tm: 8 (over z), gx: 16 (over x, y_hi, core), gy: 2 (over y_lo).
Axes of the slice: x: 4, y: 4 (y_hi: 2, y_lo: 2; y = y_hi * 2 + y_lo), z: 8, core: 2. Of those that a mesh axis runs over, the one named last changes fastest.
Arguments:
- lagrange: float32 [16, 8, 1024, 256], P('tm', None, 'gx', 'gy'), may hold values from -6 to 6
- obs_lagrange: float32 [16, 16, 2, 1024], P('tm', 'gx', 'gy'), may hold values from -6 to 6
- increment: float32 [16, 8, 1024, 256], P('tm', None, 'gx', 'gy'), may hold values from -6 to 6
- forcing: float32 [16, 8, 1024, 256], P('tm', None, 'gx', 'gy'), may hold values from -6 to 6
- departures: float32 [16, 16, 2, 1024], P('tm', 'gx', 'gy'), may hold values from -6 to 6
- model_var: float32 [16, 8, 1024, 256], P('tm', None, 'gx', 'gy'), may hold values from 0.3 to 3
- obs_var: float32 [16, 16, 2, 1024], P('tm', 'gx', 'gy'), may hold values from 0.5 to 2
- wind_east: float32 [16, 8, 1024, 256], P('tm', None, 'gx', 'gy'), may hold values from -0.3 to 0.3
- wind_north: float32 [16, 8, 1024, 256], P('tm', None, 'gx', 'gy'), may hold values from -0.3 to 0.3
- obs_cells: int32 [16, 16, 2, 1024], P('tm', 'gx', 'gy'), may hold values from 0 to 65535
- step_count: int32 [16], P('tm'), may hold values from 1 to 4, as said below
Outputs:
- lagrange_next: float32 [16, 8, 1024, 256], P('tm', None, 'gx', 'gy')
- obs_lagrange_next: float32 [16, 16, 2, 1024], P('tm', 'gx', 'gy')
- increment_next: float32 [16, 8, 1024, 256], P('tm', None, 'gx', 'gy')
- residual_model: float32 [16, 8, 1024, 256], P('tm', None, 'gx', 'gy')
- residual_obs: float32 [16, 16, 2, 1024], P('tm', 'gx', 'gy')
- residual_increment: float32 [16, 8, 1024, 256], P('tm', None, 'gx', 'gy')
Inputs may be any that keep to these rules, and one draw needn't show every extreme that they name: `step_count`: each sub-window's number of model steps; at least one sub-window takes 4.
All inputs are finite; a program needn't handle non-finite values.
Results may differ from a plain program's by a relative error of at most 0.0003.
Values sent between devices are 32-bit elements; how exact they have to be, the bound alone decides.
No kernel may reach another device: no remote copies, remote signals or barrier semaphores. Data moves between devices by JAX's collectives and lax.ppermute only.
A program may use at most 64 MiB of HBM per device.

v0:
```python
import jax
import jax.numpy as jnp
from jax import lax
from jax.sharding import PartitionSpec as P

MAXSTEP = 4


DIFFUSION = 0.18
VERTICAL = 0.1
CENTRE = 1.0 - 4.0 * DIFFUSION - 2.0 * VERTICAL


def extended_2(block, sides, width):
    for axis, dim in sides:
        count = lax.axis_size(axis)
        forward = [(i, i + 1) for i in range(count - 1)]
        backward = [(target, source) for source, target in forward]
        low = lax.ppermute(
            lax.slice_in_dim(block, block.shape[dim] - width, None, axis=dim), axis, forward
        )
        high = lax.ppermute(lax.slice_in_dim(block, 0, width, axis=dim), axis, backward)
        block = jnp.concatenate([low, block, high], axis=dim)
    return block


def passed_along(value, axis, steps):
    count = lax.axis_size(axis)
    leading, last = (max(0, -steps), min(count, count - steps))
    return lax.ppermute(value, axis, [(source, source + steps) for source in range(leading, last)])


def interior(array_in, along_x, along_y):
    return array_in[
        :,
        :,
        1 + along_x : array_in.shape[2] - 1 + along_x,
        1 + along_y : array_in.shape[3] - 1 + along_y,
    ]


def vertical_sum(field):
    padded = jnp.pad(field, ((0, 0), (1, 1), (0, 0), (0, 0)))
    return padded[:, 2:] + padded[:, :-2]


def advance(extended, coefs, counts, step_index, adjoint):
    east, west, north, south = [member for member in coefs]
    centre = interior(extended, 0, 0)
    if adjoint:
        stepped = (
            CENTRE * centre
            + interior(east, -1, 0) * interior(extended, -1, 0)
            + interior(west, 1, 0) * interior(extended, 1, 0)
            + interior(north, 0, -1) * interior(extended, 0, -1)
            + interior(south, 0, 1) * interior(extended, 0, 1)
            + VERTICAL * vertical_sum(centre)
        )
    else:
        stepped = (
            CENTRE * centre
            + interior(east, 0, 0) * interior(extended, 1, 0)
            + interior(west, 0, 0) * interior(extended, -1, 0)
            + interior(north, 0, 0) * interior(extended, 0, 1)
            + interior(south, 0, 0) * interior(extended, 0, -1)
            + VERTICAL * vertical_sum(centre)
        )
    return jnp.where(step_index < counts[:, None, None, None], stepped, centre)


def shards(
    lagrange,
    obs_lagrange,
    increment,
    forcing,
    departures,
    model_var,
    obs_var,
    wind_east,
    wind_north,
    obs_cells,
    step_count,
):
    subs, levels, rows_x, rows_y = increment.shape
    cells = levels * rows_x * rows_y
    wind_margin = 1
    winds = extended_2(jnp.stack((wind_east, wind_north)), (("gx", 3), ("gy", 4)), wind_margin)
    coefs = (
        DIFFUSION - 0.5 * winds[0],
        DIFFUSION + 0.5 * winds[0],
        DIFFUSION - 0.5 * winds[1],
        DIFFUSION + 0.5 * winds[1],
    )

    def advance_all(extended, step_index, adjoint_flags):
        sections = jnp.split(extended, len(adjoint_flags), 0)
        stepped = [
            advance(section, coefs, step_count, step_index, is_adjoint)
            for section, is_adjoint in zip(sections, adjoint_flags)
        ]
        return stepped[0]

    def sweep(field, adjoint_flags):
        for step_index in range(MAXSTEP):
            extended = extended_2(field, (("gx", 2), ("gy", 3)), 1)
            field = advance_all(extended, step_index, adjoint_flags)
        return field

    tile_base = jnp.arange(subs, dtype=jnp.int32).reshape(subs, 1, 1, 1) * cells
    flat_index = (tile_base + obs_cells).reshape(-1)

    def observe(field):
        return field.reshape(-1)[flat_index].reshape(obs_cells.shape)

    def spread(values):
        summed = jnp.zeros((subs * cells,), jnp.float32).at[flat_index].add(values.reshape(-1))
        return summed.reshape(increment.shape)

    def apply_operator(lagr, obs_lagr, incr):
        following_head = passed_along(lagr[:1], "tm", -1)
        following = jnp.concatenate((lagr[1:], following_head), 0)
        forward = sweep(incr, (False,))
        backward = sweep(following, (True,))
        arriving = passed_along(forward[-1:], "tm", 1)
        previous = jnp.concatenate((arriving, forward[:-1]), 0)
        model_part = model_var * lagr + (incr - previous)
        obs_part = obs_var * obs_lagr + observe(incr)
        incr_part = lagr - backward + spread(obs_lagr)
        return (model_part, obs_part, incr_part)

    first = apply_operator(lagrange, obs_lagrange, increment)
    resid = (forcing - first[0], departures - first[1], -first[2])
    image = apply_operator(resid[0], resid[1], resid[2])
    cross_local = (
        jnp.sum(resid[0] * image[0]) + jnp.sum(resid[1] * image[1]) + jnp.sum(resid[2] * image[2])
    )
    square_local = (
        jnp.sum(image[0] * image[0]) + jnp.sum(image[1] * image[1]) + jnp.sum(image[2] * image[2])
    )
    cross, square = lax.psum((cross_local, square_local), ("tm", "gx", "gy"))
    alpha = cross / (square + 1e-06)
    return (
        lagrange + alpha * resid[0],
        obs_lagrange + alpha * resid[1],
        increment + alpha * resid[2],
        resid[0] - alpha * image[0],
        resid[1] - alpha * image[1],
        resid[2] - alpha * image[2],
    )


def solution(mesh):
    return jax.shard_map(
        shards,
        mesh=mesh,
        in_specs=(
            P("tm", None, "gx", "gy"),
            P("tm", "gx", "gy", None),
            P("tm", None, "gx", "gy"),
            P("tm", None, "gx", "gy"),
            P("tm", "gx", "gy", None),
            P("tm", None, "gx", "gy"),
            P("tm", "gx", "gy", None),
            P("tm", None, "gx", "gy"),
            P("tm", None, "gx", "gy"),
            P("tm", "gx", "gy", None),
            P("tm"),
        ),
        out_specs=(
            P("tm", None, "gx", "gy"),
            P("tm", "gx", "gy", None),
            P("tm", None, "gx", "gy"),
            P("tm", None, "gx", "gy"),
            P("tm", "gx", "gy", None),
            P("tm", None, "gx", "gy"),
        ),
        check_vma=False,
    )
```

profile of v0, /device:TPU:1, one launch (start us, length us, event | category | flops | bytes accessed | tf_op | source)
XLA Modules:
  0.0 580.3 jit_solution(11048746948241062006)
XLA Ops:
  1.6 5.1 collective-permute-start.4
  39.0 6.0 %collective-permute-start.9 = (f32[2,8,1,128]{3,2,1,0:T(1,128)S(1)}, f32[2,8,1,128]{3,2,1,0:T(1,128)S(1)}, u32[]{:S(2)}, u32[]{:S(2)}) collective-permute-start(f32[2,8,1,128]{3,2,1,0:T(1,128)S(1)} %get-tuple-element.104), channel_id=1, source_target_pairs={{0,2},{2,4},{4,6},{6,8},{8,10},{10,12},{12,14},{14,16},{16,18},{18... | collective-permute-start | bytes 24584 | tf_op jit(solution)/shard_map/ppermute | solution.py:19
  62.2 6.5 %collective-permute-start.13 = (f32[2,8,1,128]{3,2,1,0:T(1,128)S(1)}, f32[2,8,1,128]{3,2,1,0:T(1,128)S(1)}, u32[]{:S(2)}, u32[]{:S(2)}) collective-permute-start(f32[2,8,1,128]{3,2,1,0:T(1,128)S(1)} %get-tuple-element.102), channel_id=1, source_target_pairs={{0,2},{2,4},{4,6},{6,8},{8,10},{10,12},{12,14},{14,16},{16,18},{18... | collective-permute-start | bytes 24584 | tf_op jit(solution)/shard_map/ppermute | solution.py:19
  89.6 6.3 %collective-permute-start.17 = (f32[2,8,1,128]{3,2,1,0:T(1,128)S(1)}, f32[2,8,1,128]{3,2,1,0:T(1,128)S(1)}, u32[]{:S(2)}, u32[]{:S(2)}) collective-permute-start(f32[2,8,1,128]{3,2,1,0:T(1,128)S(1)} %get-tuple-element.100), channel_id=1, source_target_pairs={{0,2},{2,4},{4,6},{6,8},{8,10},{10,12},{12,14},{14,16},{16,18},{18... | collective-permute-start | bytes 24584 | tf_op jit(solution)/shard_map/ppermute | solution.py:19
  106.7 6.3 %collective-permute-start.22 = (f32[2,8,1,128]{3,2,1,0:T(1,128)S(1)}, f32[2,8,1,128]{3,2,1,0:T(1,128)S(1)}, u32[]{:S(2)}, u32[]{:S(2)}) collective-permute-start(f32[2,8,1,128]{3,2,1,0:T(1,128)S(1)} %get-tuple-element.84), channel_id=1, source_target_pairs={{0,2},{2,4},{4,6},{6,8},{8,10},{10,12},{12,14},{14,16},{16,18},{18... | collective-permute-start | bytes 24584 | tf_op jit(solution)/shard_map/ppermute | solution.py:19
  135.5 6.2 %collective-permute-start.26 = (f32[2,8,1,128]{3,2,1,0:T(1,128)S(1)}, f32[2,8,1,128]{3,2,1,0:T(1,128)S(1)}, u32[]{:S(2)}, u32[]{:S(2)}) collective-permute-start(f32[2,8,1,128]{3,2,1,0:T(1,128)S(1)} %get-tuple-element.82), channel_id=1, source_target_pairs={{0,2},{2,4},{4,6},{6,8},{8,10},{10,12},{12,14},{14,16},{16,18},{18... | collective-permute-start | bytes 24584 | tf_op jit(solution)/shard_map/ppermute | solution.py:19
  159.2 5.0 collective-permute-start.20
  170.7 5.4 collective-permute-start.30
  186.5 8.2 %collective-permute-start.56 = (f32[2,8,1,128]{3,2,1,0:T(1,128)S(1)}, f32[2,8,1,128]{3,2,1,0:T(1,128)S(1)}, u32[]{:S(2)}, u32[]{:S(2)}) collective-permute-start(f32[2,8,1,128]{3,2,1,0:T(1,128)S(1)} %get-tuple-element.94), channel_id=1, source_target_pairs={{0,2},{2,4},{4,6},{6,8},{8,10},{10,12},{12,14},{14,16},{16,18},{18... | collective-permute-start | bytes 24584 | tf_op jit(solution)/shard_map/ppermute | solution.py:19
  222.1 7.7 %collective-permute-start.60 = (f32[2,8,1,128]{3,2,1,0:T(1,128)S(1)}, f32[2,8,1,128]{3,2,1,0:T(1,128)S(1)}, u32[]{:S(2)}, u32[]{:S(2)}) collective-permute-start(f32[2,8,1,128]{3,2,1,0:T(1,128)S(1)} %get-tuple-element.92), channel_id=1, source_target_pairs={{0,2},{2,4},{4,6},{6,8},{8,10},{10,12},{12,14},{14,16},{16,18},{18... | collective-permute-start | bytes 24584 | tf_op jit(solution)/shard_map/ppermute | solution.py:19
  231.8 11.8 %gather_fusion = f32[2048]{0:T(1024)S(1)} fusion(f32[131072]{0:T(1024)S(1)} %bitcast.21, s32[2048]{0:T(1024)S(1)} %broadcast_clamp_fusion), kind=kCustom, calls=%fused_computation | custom fusion | bytes 24576 | tf_op jit(solution)/shard_map/gather | solution.py:113
  265.1 5.7 collective-permute-start.64
  273.4 5.1 collective-permute-start.34
  295.9 7.0 %collective-permute-start.68 = (f32[2,8,1,128]{3,2,1,0:T(1,128)S(1)}, f32[2,8,1,128]{3,2,1,0:T(1,128)S(1)}, u32[]{:S(2)}, u32[]{:S(2)}) collective-permute-start(f32[2,8,1,128]{3,2,1,0:T(1,128)S(1)} %get-tuple-element.88), channel_id=1, source_target_pairs={{0,2},{2,4},{4,6},{6,8},{8,10},{10,12},{12,14},{14,16},{16,18},{18... | collective-permute-start | bytes 24584 | tf_op jit(solution)/shard_map/ppermute | solution.py:19
  316.8 5.1 collective-permute-start.70
  324.8 12.0 %scatter_custom_fusion.1 = f32[131072]{0:T(1024)} fusion(s32[2048]{0:T(1024)S(1)} %bitcast.33, f32[2048]{0:T(1024)S(1)} %bitcast.30, f32[]{:T(128)} %constant.5.clone.1), kind=kCustom, calls=%fused_computation.416 | custom fusion | flops 2048 | bytes 524292 | tf_op jit(solution)/shard_map/scatter-add | solution.py:116
  336.9 12.0 %scatter_custom_fusion = f32[131072]{0:T(1024)} fusion(s32[2048]{0:T(1024)S(1)} %bitcast.34, f32[2048]{0:T(1024)S(1)} %bitcast.31, f32[]{:T(128)} %constant.5.clone.1), kind=kCustom, calls=%fused_computation.418 | custom fusion | flops 2048 | bytes 524292 | tf_op jit(solution)/shard_map/scatter-add | solution.py:116
  355.5 8.6 %multiply_reduce_fusion = (f32[]{:T(128)}, f32[]{:T(128)}, f32[2,8,64,128]{3,2,1,0:T(8,128)}, f32[2,8,64,128]{3,2,1,0:T(8,128)S(1)}) fusion(f32[2,8,64,128]{3,2,1,0:T(8,128)} %bitcast.28, f32[2,8,64,128]{3,2,1,0:T(8,128)} %copy-done.3, f32[2,8,64,128]{3,2,1,0:T(8,128)} %copy-done.11, f32[2,8,66,1]{3,2,1,0:T(8,128)} %copy.108, ...), kind=kLoop, calls=%fused_computation.412 | loop fusion | flops 6684670 | bytes 6341130 | tf_op jit(solution)/shard_map/reduce_sum | solution.py:138
  366.0 6.9 %collective-permute-start.39 = (f32[2,8,1,128]{3,2,1,0:T(1,128)S(1)}, f32[2,8,1,128]{3,2,1,0:T(1,128)S(1)}, u32[]{:S(2)}, u32[]{:S(2)}) collective-permute-start(f32[2,8,1,128]{3,2,1,0:T(1,128)S(1)} %get-tuple-element.76), channel_id=1, source_target_pairs={{0,2},{2,4},{4,6},{6,8},{8,10},{10,12},{12,14},{14,16},{16,18},{18... | collective-permute-start | bytes 24584 | tf_op jit(solution)/shard_map/ppermute | solution.py:19
  390.2 6.6 %collective-permute-start.43 = (f32[2,8,1,128]{3,2,1,0:T(1,128)S(1)}, f32[2,8,1,128]{3,2,1,0:T(1,128)S(1)}, u32[]{:S(2)}, u32[]{:S(2)}) collective-permute-start(f32[2,8,1,128]{3,2,1,0:T(1,128)S(1)} %get-tuple-element.74), channel_id=1, source_target_pairs={{0,2},{2,4},{4,6},{6,8},{8,10},{10,12},{12,14},{14,16},{16,18},{18... | collective-permute-start | bytes 24584 | tf_op jit(solution)/shard_map/ppermute | solution.py:19
  415.4 7.2 %collective-permute-start.47 = (f32[2,8,1,128]{3,2,1,0:T(1,128)S(1)}, f32[2,8,1,128]{3,2,1,0:T(1,128)S(1)}, u32[]{:S(2)}, u32[]{:S(2)}) collective-permute-start(f32[2,8,1,128]{3,2,1,0:T(1,128)S(1)} %get-tuple-element.72), channel_id=1, source_target_pairs={{0,2},{2,4},{4,6},{6,8},{8,10},{10,12},{12,14},{14,16},{16,18},{18... | collective-permute-start | bytes 24584 | tf_op jit(solution)/shard_map/ppermute | solution.py:19
  441.5 6.8 %collective-permute-start.51 = (f32[2,8,1,128]{3,2,1,0:T(1,128)S(1)}, f32[2,8,1,128]{3,2,1,0:T(1,128)S(1)}, u32[]{:S(2)}, u32[]{:S(2)}) collective-permute-start(f32[2,8,1,128]{3,2,1,0:T(1,128)S(1)} %get-tuple-element.70), channel_id=1, source_target_pairs={{0,2},{2,4},{4,6},{6,8},{8,10},{10,12},{12,14},{14,16},{16,18},{18... | collective-permute-start | bytes 24584 | tf_op jit(solution)/shard_map/ppermute | solution.py:19
  468.0 11.8 %gather_fusion.1 = f32[2048]{0:T(1024)S(1)} fusion(f32[131072]{0:T(1024)S(1)} %bitcast.20, s32[2048]{0:T(1024)S(1)} %broadcast_clamp_fusion), kind=kCustom, calls=%fused_computation.1 | custom fusion | bytes 24576 | tf_op jit(solution)/shard_map/gather | solution.py:113
  487.6 88.0 %all-reduce.16 = (f32[]{:T(128)}, f32[]{:T(128)}) all-reduce(f32[]{:T(128)S(6)} %add.513, f32[]{:T(128)S(6)} %add.515), channel_id=1, replica_groups=mesh['tm'=8,'gx'=16,'gy'=2] {'tm','gx','gy'}, use_global_device_ids=true, to_apply=%region_5.6 | all-reduce | flops 2 | bytes 16 | tf_op jit(solution)/shard_map/psum | solution.py:140
  (360 shorter events, 315.3 us)
Async XLA Ops:
  1.6 13.5 %collective-permute-start.4 = (f32[2,8,1,128]{3,2,1,0:T(1,128)S(1)}, f32[2,8,1,128]{3,2,1,0:T(1,128)S(1)}, u32[]{:S(2)}, u32[]{:S(2)}) collective-permute-start(f32[2,8,1,128]{3,2,1,0:T(1,128)S(1)} %get-tuple-element.107), channel_id=1, source_target_pairs={{2,0},{4,2},{6,4},{8,6},{10,8},{12,10},{14,12},{16,14},{18,16},{20... | collective-permute-start | bytes 24584 | tf_op jit(solution)/shard_map/ppermute | solution.py:22
  10.7 10.6 %collective-permute-start = (f32[2,2,8,1,128]{4,3,2,1,0:T(1,128)S(1)}, f32[2,2,8,1,128]{4,3,2,1,0:T(1,128)S(1)}, u32[]{:S(2)}, u32[]{:S(2)}) collective-permute-start(f32[2,2,8,1,128]{4,3,2,1,0:T(1,128)S(1)} %get-tuple-element.30), channel_id=1, source_target_pairs={{0,2},{2,4},{4,6},{6,8},{8,10},{10,12},{12,14},{14,16},{16,18},{18... | collective-permute-start | bytes 49160 | tf_op jit(solution)/shard_map/ppermute | solution.py:19
  15.6 12.1 %collective-permute-start.6 = (f32[2,8,66,1]{2,1,3,0:T(8,128)S(1)}, f32[2,8,66,1]{2,1,3,0:T(8,128)S(1)}, u32[]{:S(2)}, u32[]{:S(2)}) collective-permute-start(f32[2,8,66,1]{2,1,3,0:T(8,128)S(1)} %copy.45), channel_id=1, source_target_pairs={{1,0},{3,2},{5,4},{7,6},{9,8},{11,10},{13,12},{15,14},{17,16},{19,... | collective-permute-start | bytes 12680 | tf_op jit(solution)/shard_map/ppermute | solution.py:22
  17.3 11.5 %collective-permute-start.7 = (f32[2,8,66,1]{2,1,3,0:T(8,128)S(1)}, f32[2,8,66,1]{2,1,3,0:T(8,128)S(1)}, u32[]{:S(2)}, u32[]{:S(2)}) collective-permute-start(f32[2,8,66,1]{2,1,3,0:T(8,128)S(1)} %copy.47), channel_id=1, source_target_pairs={{0,1},{2,3},{4,5},{6,7},{8,9},{10,11},{12,13},{14,15},{16,17},{18,... | collective-permute-start | bytes 12680 | tf_op jit(solution)/shard_map/ppermute | solution.py:19
  79.6 26.3 %collective-permute-start.21 = (f32[1,8,64,128]{3,2,1,0:T(8,128)}, f32[1,8,64,128]{3,2,1,0:T(8,128)}, u32[]{:S(2)}, u32[]{:S(2)}) collective-permute-start(f32[1,8,64,128]{3,2,1,0:T(8,128)} %get-tuple-element.87), channel_id=1, source_target_pairs={{32,0},{64,32},{96,64},{128,96},{160,128},{192,160},{224,192},{33,... | collective-permute-start | bytes 786440 | tf_op jit(solution)/shard_map/ppermute | solution.py:30
  99.2 15.7 %collective-permute-start.18 = (f32[2,8,66,1]{2,1,3,0:T(8,128)S(1)}, f32[2,8,66,1]{2,1,3,0:T(8,128)S(1)}, u32[]{:S(2)}, u32[]{:S(2)}) collective-permute-start(f32[2,8,66,1]{2,1,3,0:T(8,128)S(1)} %copy.57), channel_id=1, source_target_pairs={{1,0},{3,2},{5,4},{7,6},{9,8},{11,10},{13,12},{15,14},{17,16},{19,... | collective-permute-start | bytes 12680 | tf_op jit(solution)/shard_map/ppermute | solution.py:22
  101.8 14.2 %collective-permute-start.19 = (f32[2,8,66,1]{2,1,3,0:T(8,128)S(1)}, f32[2,8,66,1]{2,1,3,0:T(8,128)S(1)}, u32[]{:S(2)}, u32[]{:S(2)}) collective-permute-start(f32[2,8,66,1]{2,1,3,0:T(8,128)S(1)} %copy.59), channel_id=1, source_target_pairs={{0,1},{2,3},{4,5},{6,7},{8,9},{10,11},{12,13},{14,15},{16,17},{18,... | collective-permute-start | bytes 12680 | tf_op jit(solution)/shard_map/ppermute | solution.py:19
  135.5 11.8 %collective-permute-start.26 = (f32[2,8,1,128]{3,2,1,0:T(1,128)S(1)}, f32[2,8,1,128]{3,2,1,0:T(1,128)S(1)}, u32[]{:S(2)}, u32[]{:S(2)}) collective-permute-start(f32[2,8,1,128]{3,2,1,0:T(1,128)S(1)} %get-tuple-element.82), channel_id=1, source_target_pairs={{0,2},{2,4},{4,6},{6,8},{8,10},{10,12},{12,14},{14,16},{16,18},{18... | collective-permute-start | bytes 24584 | tf_op jit(solution)/shard_map/ppermute | solution.py:19
  151.3 12.9 %collective-permute-start.28 = (f32[2,8,66,1]{2,1,3,0:T(8,128)S(1)}, f32[2,8,66,1]{2,1,3,0:T(8,128)S(1)}, u32[]{:S(2)}, u32[]{:S(2)}) collective-permute-start(f32[2,8,66,1]{2,1,3,0:T(8,128)S(1)} %copy.65), channel_id=1, source_target_pairs={{0,1},{2,3},{4,5},{6,7},{8,9},{10,11},{12,13},{14,15},{16,17},{18,... | collective-permute-start | bytes 12680 | tf_op jit(solution)/shard_map/ppermute | solution.py:19
  159.2 18.9 %collective-permute-start.20 = (f32[1,8,64,128]{3,2,1,0:T(8,128)}, f32[1,8,64,128]{3,2,1,0:T(8,128)}, u32[]{:S(2)}, u32[]{:S(2)}) collective-permute-start(f32[1,8,64,128]{3,2,1,0:T(8,128)} %get-tuple-element.98), channel_id=1, source_target_pairs={{0,32},{32,64},{64,96},{96,128},{128,160},{160,192},{192,224},{1,3... | collective-permute-start | bytes 786440 | tf_op jit(solution)/shard_map/ppermute | solution.py:30
  186.5 18.2 %collective-permute-start.56 = (f32[2,8,1,128]{3,2,1,0:T(1,128)S(1)}, f32[2,8,1,128]{3,2,1,0:T(1,128)S(1)}, u32[]{:S(2)}, u32[]{:S(2)}) collective-permute-start(f32[2,8,1,128]{3,2,1,0:T(1,128)S(1)} %get-tuple-element.94), channel_id=1, source_target_pairs={{0,2},{2,4},{4,6},{6,8},{8,10},{10,12},{12,14},{14,16},{16,18},{18... | collective-permute-start | bytes 24584 | tf_op jit(solution)/shard_map/ppermute | solution.py:19
  199.1 44.5 %collective-permute-start.32 = (f32[2,8,66,1]{2,1,3,0:T(8,128)S(1)}, f32[2,8,66,1]{2,1,3,0:T(8,128)S(1)}, u32[]{:S(2)}, u32[]{:S(2)}) collective-permute-start(f32[2,8,66,1]{2,1,3,0:T(8,128)S(1)} %copy.69), channel_id=1, source_target_pairs={{0,1},{2,3},{4,5},{6,7},{8,9},{10,11},{12,13},{14,15},{16,17},{18,... | collective-permute-start | bytes 12680 | tf_op jit(solution)/shard_map/ppermute | solution.py:19
  203.4 41.3 %collective-permute-start.33 = (f32[2,8,66,1]{2,1,3,0:T(8,128)S(1)}, f32[2,8,66,1]{2,1,3,0:T(8,128)S(1)}, u32[]{:S(2)}, u32[]{:S(2)}) collective-permute-start(f32[2,8,66,1]{2,1,3,0:T(8,128)S(1)} %copy.71), channel_id=1, source_target_pairs={{1,0},{3,2},{5,4},{7,6},{9,8},{11,10},{13,12},{15,14},{17,16},{19,... | collective-permute-start | bytes 12680 | tf_op jit(solution)/shard_map/ppermute | solution.py:22
  222.1 23.7 %collective-permute-start.60 = (f32[2,8,1,128]{3,2,1,0:T(1,128)S(1)}, f32[2,8,1,128]{3,2,1,0:T(1,128)S(1)}, u32[]{:S(2)}, u32[]{:S(2)}) collective-permute-start(f32[2,8,1,128]{3,2,1,0:T(1,128)S(1)} %get-tuple-element.92), channel_id=1, source_target_pairs={{0,2},{2,4},{4,6},{6,8},{8,10},{10,12},{12,14},{14,16},{16,18},{18... | collective-permute-start | bytes 24584 | tf_op jit(solution)/shard_map/ppermute | solution.py:19
  229.9 16.0 %collective-permute-start.61 = (f32[2,8,1,128]{3,2,1,0:T(1,128)S(1)}, f32[2,8,1,128]{3,2,1,0:T(1,128)S(1)}, u32[]{:S(2)}, u32[]{:S(2)}) collective-permute-start(f32[2,8,1,128]{3,2,1,0:T(1,128)S(1)} %get-tuple-element.93), channel_id=1, source_target_pairs={{2,0},{4,2},{6,4},{8,6},{10,8},{12,10},{14,12},{16,14},{18,16},{20... | collective-permute-start | bytes 24584 | tf_op jit(solution)/shard_map/ppermute | solution.py:22
  265.1 15.3 %collective-permute-start.64 = (f32[2,8,1,128]{3,2,1,0:T(1,128)S(1)}, f32[2,8,1,128]{3,2,1,0:T(1,128)S(1)}, u32[]{:S(2)}, u32[]{:S(2)}) collective-permute-start(f32[2,8,1,128]{3,2,1,0:T(1,128)S(1)} %get-tuple-element.90), channel_id=1, source_target_pairs={{0,2},{2,4},{4,6},{6,8},{8,10},{10,12},{12,14},{14,16},{16,18},{18... | collective-permute-start | bytes 24584 | tf_op jit(solution)/shard_map/ppermute | solution.py:19
  273.4 13.1 %collective-permute-start.34 = (f32[2,8,1,128]{3,2,1,0:T(1,128)}, f32[2,8,1,128]{3,2,1,0:T(1,128)S(1)}, u32[]{:S(2)}, u32[]{:S(2)}) collective-permute-start(f32[2,8,1,128]{3,2,1,0:T(1,128)} %get-tuple-element.78), channel_id=1, source_target_pairs={{0,2},{2,4},{4,6},{6,8},{8,10},{10,12},{12,14},{14,16},{16,18},{18... | collective-permute-start | bytes 24584 | tf_op jit(solution)/shard_map/ppermute | solution.py:19
  295.9 17.8 %collective-permute-start.68 = (f32[2,8,1,128]{3,2,1,0:T(1,128)S(1)}, f32[2,8,1,128]{3,2,1,0:T(1,128)S(1)}, u32[]{:S(2)}, u32[]{:S(2)}) collective-permute-start(f32[2,8,1,128]{3,2,1,0:T(1,128)S(1)} %get-tuple-element.88), channel_id=1, source_target_pairs={{0,2},{2,4},{4,6},{6,8},{8,10},{10,12},{12,14},{14,16},{16,18},{18... | collective-permute-start | bytes 24584 | tf_op jit(solution)/shard_map/ppermute | solution.py:19
  302.9 10.8 %collective-permute-start.69 = (f32[2,8,1,128]{3,2,1,0:T(1,128)S(1)}, f32[2,8,1,128]{3,2,1,0:T(1,128)S(1)}, u32[]{:S(2)}, u32[]{:S(2)}) collective-permute-start(f32[2,8,1,128]{3,2,1,0:T(1,128)S(1)} %get-tuple-element.89), channel_id=1, source_target_pairs={{2,0},{4,2},{6,4},{8,6},{10,8},{12,10},{14,12},{16,14},{18,16},{20... | collective-permute-start | bytes 24584 | tf_op jit(solution)/shard_map/ppermute | solution.py:22
  308.0 40.9 %collective-permute-start.36 = (f32[2,8,66,1]{2,1,3,0:T(8,128)}, f32[2,8,66,1]{2,1,3,0:T(8,128)}, u32[]{:S(2)}, u32[]{:S(2)}) collective-permute-start(f32[2,8,66,1]{2,1,3,0:T(8,128)} %copy.73), channel_id=1, source_target_pairs={{0,1},{2,3},{4,5},{6,7},{8,9},{10,11},{12,13},{14,15},{16,17},{18,... | collective-permute-start | bytes 12680 | tf_op jit(solution)/shard_map/ppermute | solution.py:19
  312.5 38.2 %collective-permute-start.37 = (f32[2,8,66,1]{2,1,3,0:T(8,128)}, f32[2,8,66,1]{2,1,3,0:T(8,128)}, u32[]{:S(2)}, u32[]{:S(2)}) collective-permute-start(f32[2,8,66,1]{2,1,3,0:T(8,128)} %copy.75), channel_id=1, source_target_pairs={{1,0},{3,2},{5,4},{7,6},{9,8},{11,10},{13,12},{15,14},{17,16},{19,... | collective-permute-start | bytes 12680 | tf_op jit(solution)/shard_map/ppermute | solution.py:22
  316.8 35.7 %collective-permute-start.70 = (f32[2,8,66,1]{2,1,3,0:T(8,128)}, f32[2,8,66,1]{2,1,3,0:T(8,128)}, u32[]{:S(2)}, u32[]{:S(2)}) collective-permute-start(f32[2,8,66,1]{2,1,3,0:T(8,128)} %copy.105), channel_id=1, source_target_pairs={{0,1},{2,3},{4,5},{6,7},{8,9},{10,11},{12,13},{14,15},{16,17},{18,... | collective-permute-start | bytes 12680 | tf_op jit(solution)/shard_map/ppermute | solution.py:19
  322.8 31.5 %collective-permute-start.71 = (f32[2,8,66,1]{2,1,3,0:T(8,128)}, f32[2,8,66,1]{2,1,3,0:T(8,128)S(1)}, u32[]{:S(2)}, u32[]{:S(2)}) collective-permute-start(f32[2,8,66,1]{2,1,3,0:T(8,128)} %copy.107), channel_id=1, source_target_pairs={{1,0},{3,2},{5,4},{7,6},{9,8},{11,10},{13,12},{15,14},{17,16},{19,... | collective-permute-start | bytes 12680 | tf_op jit(solution)/shard_map/ppermute | solution.py:22
  465.1 15.4 %collective-permute-start.54 = (f32[1,8,64,128]{3,2,1,0:T(8,128)S(1)}, f32[1,8,64,128]{3,2,1,0:T(8,128)S(1)}, u32[]{:S(2)}, u32[]{:S(2)}) collective-permute-start(f32[1,8,64,128]{3,2,1,0:T(8,128)S(1)} %get-tuple-element.68), channel_id=1, source_target_pairs={{0,32},{32,64},{64,96},{96,128},{128,160},{160,192},{192,224},{1,3... | collective-permute-start | bytes 786440 | tf_op jit(solution)/shard_map/ppermute | solution.py:30
  (89 other events, 1183.3 us)
where the time goes:
time: 592 us; the launch traced here: 580 us
  starting transfers between devices  232 us (39%)
  local copies, waits for them, and re-layouts  131 us (22%)
  other arithmetic  104 us (18%)
  blocking collectives  88 us (15%)
  waiting for transfers between devices  17.5 us (3%)
  between operations  7.57 us (1%)
    ppermute x34, starting transfers between devices, extended_2(): lax.ppermute(lax.slice_in_dim(block, block.shape[dim] - width, None, axis...  162 us
    psum x1, blocking collectives, shards(): cross, square = lax.psum((cross_local, square_local), ('tm', 'gx', 'gy'))  88 us
    ppermute x34, starting transfers between devices, extended_2(): lax.ppermute(lax.slice_in_dim(block, 0, width, axis=dim), axis, backward)  59.7 us
    select_n x14, other arithmetic, advance(): return jnp.where(step_index < counts[:, None, None, None], stepped, centre)  52.9 us
    slice x40, local copies, waits for them, and re-layouts, extended_2(): lax.slice_in_dim(block, block.shape[dim] - width, None, axis=dim)  34.5 us
    slice x25, local copies, waits for them, and re-layouts, extended_2(): lax.slice_in_dim(block, 0, width, axis=dim)  28.6 us
    scatter-add x2, other arithmetic, spread(): jnp.zeros((subs * cells,), jnp.float32).at[flat_index]  24.1 us
    gather x2, local copies, waits for them, and re-layouts, observe(): return field.reshape(-1)[flat_index].reshape(obs_cells.shape)  23.6 us
  transfers between devices with their start and end apart: 72, of which 14 were waited for; matrix products, arithmetic and copies ran while one was open for 25% of the time, Pallas kernels for 0%

commit v1 on v0

v1 whole, which is shorter than its diff:
```python
import functools

import jax
import jax.numpy as jnp
from jax import lax
from jax.experimental import pallas as pl
from jax.experimental.pallas import tpu as pltpu
from jax.sharding import PartitionSpec as P

DIFFUSION = 0.18
VERTICAL = 0.1
CENTRE = 1.0 - 4.0 * DIFFUSION - 2.0 * VERTICAL

LEV, CX, CY = 8, 64, 128
HALO = 8
EXT = CX + 2 * HALO
TOP = 8
BUF = EXT + 2 * TOP
VMEM_LIMIT = 48 * 1024 * 1024
NBLOCKS = 10 * LEV + 6
F32 = jnp.float32

VM = pl.BlockSpec(memory_space=pltpu.VMEM)
SM = pl.BlockSpec(memory_space=pltpu.SMEM)


def call(body, outs, ins, scratch=(), flops=0):
    shapes = [jax.ShapeDtypeStruct(s, F32) for s in outs]
    nbytes = 4 * sum(int(a.size) for a in ins) + 4 * sum(
        functools.reduce(lambda a, b: a * b, s, 1) for s in outs
    )
    in_specs = [SM if (a.dtype == jnp.int32 and a.size < 64) else VM for a in ins]
    return pl.pallas_call(
        body,
        out_shape=shapes,
        in_specs=in_specs,
        out_specs=[VM] * len(shapes),
        scratch_shapes=list(scratch),
        compiler_params=pltpu.CompilerParams(vmem_limit_bytes=VMEM_LIMIT),
        cost_estimate=pl.CostEstimate(flops=flops, bytes_accessed=nbytes, transcendentals=0),
    )(*ins)


def iota(shape, dim):
    return lax.broadcasted_iota(jnp.int32, shape, dim)


def split(x):
    high = x.astype(jnp.bfloat16)
    low = (x - high.astype(F32)).astype(jnp.bfloat16)
    return high, low


def one_hots(cells):
    n = cells.shape[1]
    rows = (iota((LEV * CX, n), 0) == (cells >> 7)).astype(jnp.bfloat16)
    lanes = iota((CY, n), 0) == (cells & 127)
    return rows, lanes


def scatter(rows, lanes, values):
    high, low = split(values)
    zero = jnp.zeros((), jnp.bfloat16)
    parts = jnp.concatenate(
        [jnp.where(lanes, high.astype(F32), 0.0), jnp.where(lanes, low.astype(F32), 0.0)], 0
    ).astype(jnp.bfloat16)
    both = lax.dot_general(
        rows, parts, (((1,), (1,)), ((), ())), preferred_element_type=F32
    )
    return both[:, :CY] + both[:, CY:]


def gather(rows, lanes, field):
    high, low = split(field)
    both = lax.dot_general(
        jnp.concatenate([high, low], 1), rows, (((0,), (0,)), ((), ())),
        preferred_element_type=F32,
    )
    picked = both[:CY] + both[CY:]
    return jnp.sum(jnp.where(lanes, picked, 0.0), 0, keepdims=True)


def swap_halves(x):
    inner = (iota(x.shape, x.ndim - 1) & 15) < 8
    axis = x.ndim - 1
    return jnp.where(inner, pltpu.roll(x, CY - 8, axis), pltpu.roll(x, 8, axis))


def own_half(shape, gy):
    lane = iota(shape, len(shape) - 1) & 15
    return jnp.where(gy == 0, lane, lane ^ 8) < 8


def pack_kernel(
    cells, m, v, l, f, mv, we, wn, b_out, a_out, strip_out, z_out, lh_out, g1_out, g_s
):
    core = lax.axis_index("gx") % 2
    gy = lax.axis_index("gy")
    lane = iota((CX, CY), 1)
    for s in range(2):
        rows, lanes = one_hots(cells[s : s + 1])
        h = scatter(rows, lanes, m[s : s + 1])
        lh_out[s] = l[s] + h.reshape(LEV, CX, CY)
        g_s[s] = f[s] - mv[s] * l[s] - v[s]
    g1_out[...] = g_s[1]
    for z in range(LEV):
        for i in range(CX // 8):
            z_out[z * 8 + i] = l[0, z, 8 * i : 8 * i + 8]
            z_out[64 + z * 8 + i] = g_s[0, z, 8 * i : 8 * i + 8]
            z_out[128 + z * 8 + i] = mv[0, z, 8 * i : 8 * i + 8]

    def own(get):
        packed = jnp.zeros((CX, CY), F32)
        for z in range(LEV):
            rolled = pltpu.roll(get(z), (16 * z + 8) % CY, 1)
            packed = jnp.where((lane >> 4) == z, rolled, packed)
        return packed

    half = own_half((CX, CY), gy)
    pairs = (
        ((v, 0), (v, 1)), ((l, 0), (g_s, 0)), ((l, 1), (g_s, 1)),
        ((lh_out, 0), (lh_out, 1)), ((we, 0), (wn, 0)), ((we, 1), (wn, 1)),
    )
    for p, (one, two) in enumerate(pairs):
        first = own(lambda z, one=one: one[0][one[1], z])
        second = own(lambda z, two=two: two[0][two[1], z])
        strip_out[p] = jnp.where(half, first, swap_halves(second))
    for i in range(CX // 8):
        z_out[192 + i] = strip_out[1, 8 * i : 8 * i + 8]

    sub = iota((8, CY), 0)
    for out, top in ((b_out, core == 0), (a_out, core != 0)):
        row = jnp.where(top, 0, CX - 8)
        row = pl.multiple_of(row, 8)
        edge = pl.ds(row, 8)
        for k, field in enumerate((v, l, we, wn)):
            for s in range(2):
                out[pl.ds((2 * k + s) * LEV, LEV)] = field[s, :, edge, :]
        keep = jnp.where(top, sub, 7 - sub) < 4
        for s in range(2):
            for z in range(LEV):
                lh_edge = lh_out[s, z, edge, :]
                g_edge = pltpu.roll(g_s[s, z, edge, :], 4, 0)
                out[(8 + s) * LEV + z] = jnp.where(keep, lh_edge, g_edge)
        out[pl.ds(10 * LEV, 6)] = strip_out[:, edge, :]


def obs_kernel(cells, m, v, dep, ov, rm_out, h2_out):
    for s in range(2):
        rows, lanes = one_hots(cells[s : s + 1])
        seen = gather(rows, lanes, v[s].reshape(LEV * CX, CY))
        rm = dep[s : s + 1] - (ov[s : s + 1] * m[s : s + 1] + seen)
        rm_out[s : s + 1] = rm
        h2_out[s] = scatter(rows, lanes, rm).reshape(LEV, CX, CY)


class Place:
    def __init__(self):
        gx = lax.axis_index("gx")
        self.gy = lax.axis_index("gy")
        core = gx % 2
        self.b_row = pl.multiple_of(jnp.where(core == 0, TOP, TOP + HALO + CX), 8)
        self.a_row = pl.multiple_of(jnp.where(core == 0, TOP + HALO + CX, TOP), 8)
        self.low = jnp.where(gx == 0, 0.0, 1.0)
        self.high = jnp.where(gx == lax.axis_size("gx") - 1, 0.0, 1.0)


def clear(ref, guard_levels):
    lead = ref.shape[:-2]
    zero = jnp.zeros(lead + (TOP, CY), F32)
    ref[..., 0:TOP, :] = zero
    ref[..., BUF - TOP : BUF, :] = zero
    if guard_levels:
        full = jnp.zeros((BUF, CY), F32)
        for i in range(lead[0]):
            ref[i, 0] = full
            ref[i, LEV + 1] = full


def fill(dst, base, place, tile, b_block, a_block):
    for z in range(LEV):
        dst[base + z, TOP + HALO : TOP + HALO + CX] = tile(z)
        dst[base + z, pl.ds(place.b_row, 8)] = b_block(z)
        dst[base + z, pl.ds(place.a_row, 8)] = a_block(z)


def unpack(place, own, received):
    half = own_half(own.shape, place.gy)
    return jnp.where(half, own, received), swap_halves(jnp.where(half, received, own))


def fill_strips(first, second, place, own, got, own_b, got_b, own_a, got_a):
    mid = pl.ds(TOP + HALO, CX)
    for where, a, b in (
        (mid, own, got),
        (pl.ds(place.b_row, 8), own_b, got_b),
        (pl.ds(place.a_row, 8), own_a, got_a),
    ):
        one, two = unpack(place, a, b)
        first[where] = one
        second[where] = two


ROWS = slice(TOP, TOP + EXT)
UP = slice(TOP + 1, TOP + EXT + 1)
DOWN = slice(TOP - 1, TOP + EXT - 1)


def injected(strip, gy):
    lane = iota((EXT, CY), 1) & 15
    moved = jnp.where(gy == 0, pltpu.roll(strip, 119, 1), pltpu.roll(strip, 121, 1))
    return jnp.where(lane == jnp.where(gy == 0, 15, 0), moved, 0.0)


def coefficients(place, wind, strip, coef, scoef, adjoint):
    lane = iota((EXT, CY), 1)
    if not adjoint:
        for z in range(LEV):
            east, north = 0.5 * wind[0, z, ROWS], 0.5 * wind[1, z, ROWS]
            coef[0, z] = DIFFUSION - east
            coef[1, z] = DIFFUSION + east
            coef[2, z] = DIFFUSION - north
            coef[3, z] = DIFFUSION + north
        east, north = 0.5 * strip[0, ROWS], 0.5 * strip[1, ROWS]
        scoef[0] = DIFFUSION - east
        scoef[1] = DIFFUSION + east
        scoef[2] = DIFFUSION - north
        scoef[3] = DIFFUSION + north
        return
    inj = injected(strip[1, ROWS], place.gy)
    for z in range(LEV):
        north = wind[1, z, ROWS]
        edge = pltpu.roll(inj, (CY - 16 * z) % CY, 1)
        after = jnp.where(lane == CY - 1, edge, pltpu.roll(north, CY - 1, 1))
        before = jnp.where(lane == 0, edge, pltpu.roll(north, 1, 1))
        coef[0, z] = DIFFUSION + 0.5 * wind[0, z, UP]
        coef[1, z] = DIFFUSION - 0.5 * wind[0, z, DOWN]
        coef[2, z] = DIFFUSION + 0.5 * after
        coef[3, z] = DIFFUSION - 0.5 * before
    scoef[0] = DIFFUSION + 0.5 * strip[0, UP]
    scoef[1] = DIFFUSION - 0.5 * strip[0, DOWN]
    scoef[2] = DIFFUSION + 0.5 * pltpu.roll(strip[1, ROWS], CY - 1, 1)
    scoef[3] = DIFFUSION - 0.5 * pltpu.roll(strip[1, ROWS], 1, 1)


def store(dst, z, out, place):
    dst[z, TOP : TOP + HALO] = out[:HALO] * place.low
    dst[z, TOP + HALO : TOP + HALO + CX] = out[HALO : HALO + CX]
    dst[z, TOP + HALO + CX : TOP + EXT] = out[HALO + CX :] * place.high


def sweep(place, state, strip, coef, scoef, count):
    lane = iota((EXT, CY), 1)

    def one(step, _):
        now = step & 1
        src, dst = state.at[now], state.at[1 - now]
        ssrc, sdst = strip.at[now], strip.at[1 - now]
        own = ssrc[0, ROWS]
        inj = injected(own, place.gy)
        for z in range(LEV):
            mid = src[z + 1, ROWS]
            edge = pltpu.roll(inj, (CY - 16 * z) % CY, 1)
            after = jnp.where(lane == CY - 1, edge, pltpu.roll(mid, CY - 1, 1))
            before = jnp.where(lane == 0, edge, pltpu.roll(mid, 1, 1))
            out = (
                CENTRE * mid
                + coef[0, z] * src[z + 1, UP]
                + coef[1, z] * src[z + 1, DOWN]
                + coef[2, z] * after
                + coef[3, z] * before
                + VERTICAL * (src[z + 2, ROWS] + src[z, ROWS])
            )
            store(dst, z + 1, out, place)
        above = jnp.where(lane < CY - 16, pltpu.roll(own, CY - 16, 1), 0.0)
        below = jnp.where(lane >= 16, pltpu.roll(own, 16, 1), 0.0)
        out = (
            CENTRE * own
            + scoef[0] * ssrc[0, UP]
            + scoef[1] * ssrc[0, DOWN]
            + scoef[2] * pltpu.roll(own, CY - 1, 1)
            + scoef[3] * pltpu.roll(own, 1, 1)
            + VERTICAL * (above + below)
        )
        store(sdst, 0, out, place)
        return 0

    lax.fori_loop(0, count, one, 0)


STATE = pltpu.VMEM((2, LEV + 2, BUF, CY), F32)
STRIP = pltpu.VMEM((2, 1, BUF, CY), F32)
COEF = pltpu.VMEM((4, LEV, EXT, CY), F32)
SCOEF = pltpu.VMEM((4, EXT, CY), F32)
WIND = pltpu.VMEM((2, LEV, BUF, CY), F32)
WSTRIP = pltpu.VMEM((2, BUF, CY), F32)


def fill_winds(place, s, we, wn, bg, ag, own, got, by, ay, wind, wstrip):
    for k, field in enumerate((we, wn)):
        fill(
            wind.at[k], 0, place, lambda z, field=field: field[s, z],
            lambda z, k=k: bg[(4 + 2 * k + s) * LEV + z],
            lambda z, k=k: ag[(4 + 2 * k + s) * LEV + z],
        )
    p = 4 + s
    fill_strips(
        wstrip.at[0], wstrip.at[1], place, own[p], got[p],
        bg[10 * LEV + p], by[p], ag[10 * LEV + p], ay[p],
    )


def first_kernel(
    counts, v, l, we, wn, lh, g1, own, got, bg, ag, by, ay,
    ext_out, rv_out, f1_out,
    x_f, x_b, s_f, s_b, coef, scoef, wind, wstrip, extra, estrip,
):
    place = Place()
    clear(x_f, True)
    clear(x_b, True)
    for ref in (s_f, s_b, wind, wstrip, extra, estrip):
        clear(ref, False)

    def strips(p, first, second):
        fill_strips(
            first, second, place, own[p], got[p],
            bg[10 * LEV + p], by[p], ag[10 * LEV + p], ay[p],
        )

    fill_winds(place, 0, we, wn, bg, ag, own, got, by, ay, wind, wstrip)
    fill(
        x_b.at[0], 1, place, lambda z: l[1, z],
        lambda z: bg[3 * LEV + z], lambda z: ag[3 * LEV + z],
    )
    strips(2, s_b.at[0, 0], estrip.at[1])
    coefficients(place, wind, wstrip, coef, scoef, True)
    sweep(place, x_b, s_b, coef, scoef, counts[0])
    end = counts[0] & 1
    fill(
        extra.at[0], 0, place, lambda z: lh[0, z],
        lambda z: bg[8 * LEV + z], lambda z: ag[8 * LEV + z],
    )
    fill(
        extra.at[1], 0, place, lambda z: g1[z],
        lambda z: pltpu.roll(bg[9 * LEV + z], 4, 0),
        lambda z: pltpu.roll(ag[9 * LEV + z], 4, 0),
    )
    for z in range(LEV):
        rv = x_b[end, z + 1, ROWS] - extra[0, z, ROWS]
        ext_out[0, z] = rv
        rv_out[z] = rv[HALO : HALO + CX]
    strips(3, estrip.at[0], s_f.at[0, 0])
    ext_out[0, LEV] = s_b[end, 0, ROWS] - estrip[0, ROWS]

    for s in range(2):
        if s == 1:
            fill_winds(place, 1, we, wn, bg, ag, own, got, by, ay, wind, wstrip)
        coefficients(place, wind, wstrip, coef, scoef, False)
        fill(
            x_f.at[0], 1, place, lambda z, s=s: v[s, z],
            lambda z, s=s: bg[s * LEV + z], lambda z, s=s: ag[s * LEV + z],
        )
        if s == 0:
            strips(0, s_f.at[0, 0], estrip.at[0])
        else:
            strips(0, estrip.at[0], s_f.at[0, 0])
        sweep(place, x_f, s_f, coef, scoef, counts[s])
        end = counts[s] & 1
        for z in range(LEV):
            out = x_f[end, z + 1, ROWS]
            if s == 0:
                ext_out[1, z] = out + extra[1, z, ROWS]
            else:
                ext_out[2, z] = out
                f1_out[z] = out[HALO : HALO + CX]
        out = s_f[end, 0, ROWS]
        ext_out[1 + s, LEV] = out + estrip[1, ROWS] if s == 0 else out


def lane_sum(x):
    return functools.reduce(
        lambda a, b: a + b, [x[:, i : i + CY] for i in range(0, x.shape[1], CY)]
    )


def second_kernel(
    counts, cells, ext, we, wn, lh, own, got, bg, ag, by, ay, zt, zh,
    mv, h2, rm, ov,
    rv1_out, rl1_out, rl2_out, f21_out, b20_out, ql1_out, qv1_out, qm_out, dots_out,
    x_f, x_b, s_f, s_b, coef, scoef, wind, wstrip, extra, estrip,
):
    place = Place()
    clear(x_f, True)
    clear(x_b, True)
    for ref in (s_f, s_b, wind, wstrip, extra, estrip):
        clear(ref, False)
    tile = slice(HALO, HALO + CX)
    follows = jnp.where(lax.axis_index("tm") == lax.axis_size("tm") - 1, 0.0, 1.0)

    fill_winds(place, 1, we, wn, bg, ag, own, got, by, ay, wind, wstrip)
    coefficients(place, wind, wstrip, coef, scoef, True)

    def z_tile(base):
        return lambda z: zt[base + 8 * z : base + 8 * z + 8].reshape(CX, CY)

    fill(x_b.at[0], 1, place, z_tile(0), lambda z: zh[z], lambda z: zh[16 + z])
    fill(
        extra.at[1], 0, place, z_tile(64),
        lambda z: pltpu.roll(zh[8 + z], 4, 0), lambda z: pltpu.roll(zh[24 + z], 4, 0),
    )
    fill_strips(
        s_b.at[0, 0], estrip.at[1], place,
        zt[192:200].reshape(CX, CY), zh[36:44].reshape(CX, CY),
        zh[32], zh[33], zh[34], zh[35],
    )
    sweep(place, x_b, s_b, coef, scoef, counts[1])
    end = counts[1] & 1

    fill(
        extra.at[0], 0, place, lambda z: lh[1, z],
        lambda z: bg[9 * LEV + z], lambda z: ag[9 * LEV + z],
    )
    fill_strips(
        s_f.at[0, 0], estrip.at[0], place, own[3], got[3],
        bg[10 * LEV + 3], by[3], ag[10 * LEV + 3], ay[3],
    )
    for z in range(LEV):
        rv = x_b[end, z + 1, ROWS] - extra[0, z, ROWS]
        x_f[0, z + 1, ROWS] = rv
        rv1_out[z] = rv[tile]
        rl = (extra[1, z, ROWS] + ext[2, z]) * follows
        x_b[0, z + 1, ROWS] = rl
        rl2_out[z] = rl[tile]
    s_f[0, 0, ROWS] = s_b[end, 0, ROWS] - estrip[0, ROWS]
    s_b[0, 0, ROWS] = (estrip[1, ROWS] + ext[2, LEV]) * follows

    sweep(place, x_b, s_b, coef, scoef, counts[1])
    cross = jnp.zeros((8, CY), F32)
    square = jnp.zeros((8, CY), F32)

    def dots(r, q):
        return jnp.sum((r * q).reshape(-1, 8, CY), 0), jnp.sum((q * q).reshape(-1, 8, CY), 0)

    for z in range(LEV):
        rl1 = ext[1, z, tile]
        rl1_out[z] = rl1
        qv = rl1 - x_b[end, z + 1, TOP + HALO : TOP + HALO + CX] + h2[1, z]
        qv1_out[z] = qv
        c, q = dots(rv1_out[z], qv)
        cross, square = cross + c, square + q
    coefficients(place, wind, wstrip, coef, scoef, False)
    sweep(place, x_f, s_f, coef, scoef, counts[1])
    for z in range(LEV):
        f21_out[z] = x_f[end, z + 1, TOP + HALO : TOP + HALO + CX]

    end = counts[0] & 1
    fill_winds(place, 0, we, wn, bg, ag, own, got, by, ay, wind, wstrip)
    coefficients(place, wind, wstrip, coef, scoef, False)
    for z in range(LEV):
        x_f[0, z + 1, ROWS] = ext[0, z]
        x_b[0, z + 1, ROWS] = ext[1, z]
    s_f[0, 0, ROWS] = ext[0, LEV]
    s_b[0, 0, ROWS] = ext[1, LEV]
    sweep(place, x_f, s_f, coef, scoef, counts[0])
    for z in range(LEV):
        rl1 = ext[1, z, tile]
        ql = mv[1, z] * rl1 + rv1_out[z] - x_f[end, z + 1, TOP + HALO : TOP + HALO + CX]
        ql1_out[z] = ql
        c, q = dots(rl1, ql)
        cross, square = cross + c, square + q
    coefficients(place, wind, wstrip, coef, scoef, True)
    sweep(place, x_b, s_b, coef, scoef, counts[0])
    for z in range(LEV):
        b20_out[z] = x_b[end, z + 1, TOP + HALO : TOP + HALO + CX]

    for s in range(2):
        rows, lanes = one_hots(cells[s : s + 1])
        if s == 0:
            field = ext[0, 0:LEV, tile].reshape(LEV * CX, CY)
        else:
            field = rv1_out[...].reshape(LEV * CX, CY)
        seen = gather(rows, lanes, field)
        r = rm[s : s + 1]
        q = ov[s : s + 1] * r + seen
        qm_out[s : s + 1] = q
        c, q = lane_sum(r * q), lane_sum(q * q)
        first = iota((8, CY), 0) == 0
        cross = cross + jnp.where(first, c, 0.0)
        square = square + jnp.where(first, q, 0.0)
    dots_out[0] = cross
    dots_out[1] = square


def dots_kernel(
    z_f, z_rv, zt, rl2, f21, b20, z_own, h2, rv0, mv, dots_in, rl0_out, qv0_out, send_out
):
    follows = jnp.where(lax.axis_index("tm") == lax.axis_size("tm") - 1, 0.0, 1.0)
    starts = jnp.where(lax.axis_index("tm") == 0, 1.0, 0.0)
    cross, square = dots_in[0], dots_in[1]

    def total(x):
        return jnp.sum(x.reshape(-1, 8, CY), 0)

    for z in range(LEV):
        rl0 = z_own[64 + 8 * z : 72 + 8 * z].reshape(CX, CY) + z_f[z]
        rv = rv0[z]
        qv = rl0 - b20[z] + h2[0, z]
        rl0_out[z] = rl0
        qv0_out[z] = qv
        ql = (mv[0, z] * rl0 + rv) * starts
        rl2z = rl2[z]
        q2 = (zt[128 + 8 * z : 136 + 8 * z].reshape(CX, CY) * rl2z + z_rv[z] - f21[z]) * follows
        cross += total(rv * qv) + total(rl0 * ql) + total(rl2z * q2)
        square += total(qv * qv) + total(ql * ql) + total(q2 * q2)
    cross = jnp.sum(jnp.sum(cross, 0, keepdims=True), 1, keepdims=True)
    square = jnp.sum(jnp.sum(square, 0, keepdims=True), 1, keepdims=True)
    n = send_out.shape[0]
    lane = iota((n, CY), 1)
    send_out[...] = jnp.where(lane == 0, cross, jnp.where(lane == 1, square, 0.0))


def last_kernel(
    sums, l, m, v, mv, rl0, rl1, rv0, rv1, rm, z_f2, ql1, qv0, qv1, qm,
    l_out, m_out, v_out, a_out, b_out, c_out,
):
    total = jnp.sum(sums[...], 0, keepdims=True)
    lane = iota((1, CY), 1)
    cross = jnp.sum(jnp.where(lane == 0, total, 0.0), 1, keepdims=True)
    square = jnp.sum(jnp.where(lane == 1, total, 0.0), 1, keepdims=True)
    alpha = cross / (square + 1e-06)
    m_out[...] = m[...] + alpha * rm[...]
    b_out[...] = rm[...] - alpha * qm[...]
    for z in range(LEV):
        ql0 = mv[0, z] * rl0[z] + rv0[z] - z_f2[z]
        l_out[0, z] = l[0, z] + alpha * rl0[z]
        l_out[1, z] = l[1, z] + alpha * rl1[z]
        v_out[0, z] = v[0, z] + alpha * rv0[z]
        v_out[1, z] = v[1, z] + alpha * rv1[z]
        a_out[0, z] = rl0[z] - alpha * ql0
        a_out[1, z] = rl1[z] - alpha * ql1[z]
        c_out[0, z] = rv0[z] - alpha * qv0[z]
        c_out[1, z] = rv1[z] - alpha * qv1[z]


def shards(sizes, l4, m4, v4, f4, d4, mv4, ov4, we4, wn4, cells4, counts):
    ntm, ngx, ngy = sizes
    tile = (LEV, CX, CY)
    flat = lambda x: x.reshape(2, -1)
    m, dep, ov, cells = flat(m4), flat(d4), flat(ov4), flat(cells4)
    nobs = m.shape[1]

    def pair_b(i):
        return i - 1 if i % 2 == 0 else i + 1

    def plane(move_x, move_y):
        pairs = []
        for x in range(ngx):
            for y in range(ngy):
                to = move_x(x)
                if 0 <= to < ngx:
                    pairs.append((x * ngy + y, to * ngy + (1 - y if move_y else y)))
        return pairs

    same = lambda i: i
    pair_a = lambda i: i ^ 1
    axes = ("gx", "gy")
    down = [(i + 1, i) for i in range(ntm - 1)]
    up = [(i, i + 1) for i in range(ntm - 1)]

    b_send, a_send, own, z_send, lh, g1 = call(
        pack_kernel,
        [(NBLOCKS, 8, CY)] * 2 + [(6, CX, CY), (200, 8, CY), (2,) + tile, tile],
        [cells, m, v4, l4, f4, mv4, we4, wn4],
        [pltpu.VMEM((2,) + tile, F32)],
    )
    zt = lax.ppermute(z_send, "tm", down)
    bg = lax.ppermute(b_send, axes, plane(pair_b, False))
    got = lax.ppermute(own, axes, plane(same, True))
    by = lax.ppermute(b_send[10 * LEV :], axes, plane(pair_b, True))
    ag = lax.ppermute(a_send, axes, plane(pair_a, False))
    ay = lax.ppermute(a_send[10 * LEV :], axes, plane(pair_a, True))
    rm, h2 = call(obs_kernel, [(2, nobs), (2,) + tile], [cells, m, v4, dep, ov])

    p = 10 * LEV + 1
    z_edges = jnp.concatenate(
        [
            bg[2 * LEV : 3 * LEV], bg[8 * LEV : 9 * LEV],
            ag[2 * LEV : 3 * LEV], ag[8 * LEV : 9 * LEV],
            bg[p : p + 1], by[1:2], ag[p : p + 1], ay[1:2],
            got[1].reshape(8, 8, CY),
        ],
        0,
    )
    zh = lax.ppermute(z_edges, "tm", down)
    scratch = [
        STATE, STATE, STRIP, STRIP, COEF, SCOEF, WIND, WSTRIP,
        pltpu.VMEM((2, LEV, BUF, CY), F32), pltpu.VMEM((2, BUF, CY), F32),
    ]
    ext, rv0, f1 = call(
        first_kernel,
        [(3, LEV + 1, EXT, CY), tile, tile],
        [counts, v4, l4, we4, wn4, lh, g1, own, got, bg, ag, by, ay],
        scratch,
    )
    z_rv = lax.ppermute(rv0, "tm", down)
    z_f = lax.ppermute(f1, "tm", up)
    rv1, rl1, rl2, f21, b20, ql1, qv1, qm, dots = call(
        second_kernel,
        [tile] * 7 + [(2, nobs), (2, 8, CY)],
        [counts, cells, ext, we4, wn4, lh, own, got, bg, ag, by, ay, zt, zh, mv4, h2, rm, ov],
        scratch,
    )
    z_f2 = lax.ppermute(f21, "tm", up)
    n = ntm * ngx * ngy
    rl0, qv0, send = call(
        dots_kernel,
        [tile, tile, (n, CY)],
        [z_f, z_rv, zt, rl2, f21, b20, z_send, h2, rv0, mv4, dots],
    )
    sums = lax.all_to_all(send, ("tm", "gx", "gy"), 0, 0, tiled=True)
    l_next, m_next, v_next, res_l, res_m, res_v = call(
        last_kernel,
        [l4.shape, (2, nobs), v4.shape, l4.shape, (2, nobs), v4.shape],
        [sums, l4, m, v4, mv4, rl0, rl1, rv0, rv1, rm, z_f2, ql1, qv0, qv1, qm],
    )
    return l_next, m_next.reshape(m4.shape), v_next, res_l, res_m.reshape(m4.shape), res_v


def solution(mesh):
    field = P("tm", None, "gx", "gy")
    obs = P("tm", "gx", "gy", None)
    sizes = tuple(mesh.shape[a] for a in ("tm", "gx", "gy"))
    return jax.shard_map(
        functools.partial(shards, sizes),
        mesh=mesh,
        in_specs=(field, obs, field, field, obs, field, obs, field, field, obs, P("tm")),
        out_specs=(field, obs, field, field, obs, field),
        check_vma=False,
    )
```

time: 592 us -> 105 us (0.18); the launches traced: 580 us -> 104 us
  starting transfers between devices: 232 us -> 21.8 us
  local copies, waits for them, and re-layouts: 131 us -> 12 us
  other arithmetic: 104 us -> 0 us
  blocking collectives: 88 us -> 27.7 us
  Pallas kernels: 0 us -> 20 us
  between operations: 7.57 us -> 0.94 us
    ppermute x72 -> x10, starting transfers between devices: 232 us -> 21.8 us  [the longest x1 6.22 us: shards(): bg = lax.ppermute(b_send, axes, plane(pair_b, False))]
    psum x1 -> x0, blocking collectives: 88 us -> none  [shards(): cross, square = lax.psum((cross_local, square_local), ('tm', 'gx', 'gy'))]
    slice x69 -> x2, local copies, waits for them, and re-layouts: 65.9 us -> 0.01 us  [the longest x1 0.01 us: shards(): ay = lax.ppermute(a_send[10 * LEV:], axes, plane(pair_a, True))]
    select_n x15 -> x0, other arithmetic: 52.9 us -> none  [the longest x14 52.9 us: advance(): return jnp.where(step_index < counts[:, None, None, None], stepped, centre)]
    ppermute x34 -> x0, local copies, waits for them, and re-layouts: 39.4 us -> none  [the longest x17 19.7 us: extended_2(): lax.ppermute(lax.slice_in_dim(block, 0, width, axis=dim), axis, backward)]
    all_to_all x0 -> x1, blocking collectives: none -> 27.7 us  [shards(): sums = lax.all_to_all(send, ('tm', 'gx', 'gy'), 0, 0, tiled=True)]
    scatter-add x2 -> x0, other arithmetic: 24.1 us -> none  [spread(): jnp.zeros((subs * cells,), jnp.float32).at[flat_index]]
    gather x2 -> x0, local copies, waits for them, and re-layouts: 23.6 us -> none  [observe(): return field.reshape(-1)[flat_index].reshape(obs_cells.shape)]
  transfers between devices with their start and end apart: 72 -> 10, of which waited for: 14 -> 2; matrix products, arithmetic and copies ran while one was open for 25% -> 0% of each run, Pallas kernels for 0% -> 16%
where the time goes in v1:
time: 105 us; the launch traced here: 104 us
  blocking collectives  27.7 us (26%)
  starting transfers between devices  21.8 us (21%)
  waiting for transfers between devices  21.5 us (20%)
  Pallas kernels  20 us (19%)
  local copies, waits for them, and re-layouts  12 us (11%)
    all_to_all x1, blocking collectives, shards(): sums = lax.all_to_all(send, ('tm', 'gx', 'gy'), 0, 0, tiled=True)  27.7 us
    pallas_call x6, Pallas kernels, call(): pl.pallas_call(body, out_shape=shapes, in_specs=in_specs, out_specs=[VM]...  20 us
    ppermute x1, waiting for transfers between devices, shards(): zh = lax.ppermute(z_edges, 'tm', down)  14.3 us
    unnamed x45, local copies, waits for them, and re-layouts  12 us
    ppermute x1, waiting for transfers between devices, shards(): ay = lax.ppermute(a_send[10 * LEV:], axes, plane(pair_a, True))  7.23 us
    ppermute x1, starting transfers between devices, shards(): bg = lax.ppermute(b_send, axes, plane(pair_b, False))  6.22 us
    ppermute x1, starting transfers between devices, shards(): by = lax.ppermute(b_send[10 * LEV:], axes, plane(pair_b, True))  3.3 us
    ppermute x1, starting transfers between devices, shards(): z_f2 = lax.ppermute(f21, 'tm', up)  3.14 us
  transfers between devices with their start and end apart: 10, of which 2 were waited for; matrix products, arithmetic and copies ran while one was open for 0% of the time, Pallas kernels for 16%

profile of v1, /device:TPU:1, one launch (start us, length us, event | category | flops | bytes accessed | tf_op | source)
XLA Modules:
  0.0 104.0 jit_solution(16256285640658564344)
XLA Ops:
  2.1 1.0 copy-done
  3.1 1.0 copy-done.2
  4.1 1.0 copy-done.4
  5.2 1.0 copy-done.6
  6.2 1.0 copy-done.8
  7.3 1.0 copy-done.13
  8.3 1.5 %shard_map.154 = (f32[86,8,128]{2,1,0:T(8,128)S(1)}, f32[86,8,128]{2,1,0:T(8,128)S(1)}, f32[6,64,128]{2,1,0:T(8,128)S(1)}, f32[200,8,128]{2,1,0:T(8,128)S(1)}, f...) custom-call(s32[2,1024]{1,0:T(2,128)S(1)} %bitcast.21, f32[2,1024]{1,0:T(2,128)S(1)} %get-tuple-element.77.m, ...), custom_call_target="tpu_custom_call" | custom-call | bytes 5668864 | tf_op jit(solution)/shard_map/pallas_call | solution.py:33
  9.9 6.2 %collective-permute-start.1 = (f32[86,8,128]{2,1,0:T(8,128)S(1)}, f32[86,8,128]{2,1,0:T(8,128)S(1)}, u32[]{:S(2)}, u32[]{:S(2)}) collective-permute-start(f32[86,8,128]{2,1,0:T(8,128)S(1)} %get-tuple-element.38), channel_id=1, source_target_pairs={{2,4},{3,5},{4,2},{5,3},{6,8},{7,9},{8,6},{9,7},{10,12},{11,13},{1... | collective-permute-start | bytes 1056776 | tf_op jit(solution)/shard_map/ppermute | solution.py:577
  16.7 1.6 %collective-permute-start.4 = (f32[6,8,128]{2,1,0:T(8,128)S(1)}, f32[6,8,128]{2,1,0:T(8,128)S(1)}, u32[]{:S(2)}, u32[]{:S(2)}) collective-permute-start(f32[6,8,128]{2,1,0:T(8,128)S(1)} %slice.34), channel_id=1, source_target_pairs={{0,3},{1,2},{2,1},{3,0},{4,7},{5,6},{6,5},{7,4},{8,11},{9,10},{10,... | collective-permute-start | bytes 73736 | tf_op jit(solution)/shard_map/ppermute | solution.py:581
  18.3 3.3 %collective-permute-start.3 = (f32[6,8,128]{2,1,0:T(8,128)S(1)}, f32[6,8,128]{2,1,0:T(8,128)S(1)}, u32[]{:S(2)}, u32[]{:S(2)}) collective-permute-start(f32[6,8,128]{2,1,0:T(8,128)S(1)} %slice.33), channel_id=1, source_target_pairs={{2,5},{3,4},{4,3},{5,2},{6,9},{7,8},{8,7},{9,6},{10,13},{11,12},{1... | collective-permute-start | bytes 73736 | tf_op jit(solution)/shard_map/ppermute | solution.py:579
  21.6 7.2 %collective-permute-done.4.ay = f32[6,8,128]{2,1,0:T(8,128)S(1)} collective-permute-done((f32[6,8,128]{2,1,0:T(8,128)S(1)}, f32[6,8,128]{2,1,0:T(8,128)S(1)}, u32[]{:S(2)}, u32[]{:S(2)}) %collective-permute-start.4) | collective-permute-done | bytes 24608 | tf_op jit(solution)/shard_map/ppermute | solution.py:581
  28.9 1.3 %collective-permute-start.7 = (f32[200,8,128]{2,1,0:T(8,128)S(1)}, f32[200,8,128]{2,1,0:T(8,128)S(1)}, u32[]{:S(2)}, u32[]{:S(2)}) collective-permute-start(f32[200,8,128]{2,1,0:T(8,128)S(1)} %get-tuple-element.42.z_own), channel_id=1, source_target_pairs={{32,0},{64,32},{96,64},{128,96},{160,128},{192,160},{224,192},{33,... | collective-permute-start | bytes 2457608 | tf_op jit(solution)/shard_map/ppermute | solution.py:576
  30.2 5.1 %shard_map.155 = (f32[3,9,80,128]{3,2,1,0:T(8,128)S(1)}, f32[8,64,128]{2,1,0:T(8,128)S(1)}, f32[8,64,128]{2,1,0:T(8,128)S(1)}) custom-call(s32[2]{0:T(128)S(1)} %copy-done.14, f32[2,8,64,128]{3,2,1,0:T(8,128)S(1)} %copy-done.1, f32[2,8,64,128]{3,2,1,0:T(8,128)S(1)} %copy-done.8, f32[2,8,64,128]{3,2,1,0:T(8,128)S(1)} %copy-done.5, ...), custom_call_target="tpu_custom_call" | custom-call | bytes 5660680 | tf_op jit(solution)/shard_map/pallas_call | solution.py:33
  35.3 1.0 copy-done.12
  36.3 3.0 %collective-permute-start.5 = (f32[8,64,128]{2,1,0:T(8,128)S(1)}, f32[8,64,128]{2,1,0:T(8,128)S(1)}, u32[]{:S(2)}, u32[]{:S(2)}) collective-permute-start(f32[8,64,128]{2,1,0:T(8,128)S(1)} %get-tuple-element.40), channel_id=1, source_target_pairs={{0,32},{32,64},{64,96},{96,128},{128,160},{160,192},{192,224},{1,3... | collective-permute-start | bytes 786440 | tf_op jit(solution)/shard_map/ppermute | solution.py:606
  39.4 1.3 %collective-permute-start.6 = (f32[8,64,128]{2,1,0:T(8,128)S(1)}, f32[8,64,128]{2,1,0:T(8,128)S(1)}, u32[]{:S(2)}, u32[]{:S(2)}) collective-permute-start(f32[8,64,128]{2,1,0:T(8,128)S(1)} %get-tuple-element.41.rv0), channel_id=1, source_target_pairs={{32,0},{64,32},{96,64},{128,96},{160,128},{192,160},{224,192},{33,... | collective-permute-start | bytes 786440 | tf_op jit(solution)/shard_map/ppermute | solution.py:605
  40.8 1.3 %collective-permute-start.8 = (f32[44,8,128]{2,1,0:T(8,128)S(1)}, f32[44,8,128]{2,1,0:T(8,128)S(1)}, u32[]{:S(2)}, u32[]{:S(2)}) collective-permute-start(f32[44,8,128]{2,1,0:T(8,128)S(1)} %fusion), channel_id=1, source_target_pairs={{32,0},{64,32},{96,64},{128,96},{160,128},{192,160},{224,192},{33,... | collective-permute-start | bytes 540680 | tf_op jit(solution)/shard_map/ppermute | solution.py:594
  42.1 2.4 %shard_map.156 = (f32[2,1024]{1,0:T(2,128)S(1)}, f32[2,8,64,128]{3,2,1,0:T(8,128)S(1)}) custom-call(s32[2,1024]{1,0:T(2,128)S(1)} %bitcast.22, f32[2,1024]{1,0:T(2,128)S(1)} %get-tuple-element.77.m, f32[2,8,64,128]{3,2,1,0:T(8,128)S(1)} %copy-done.1, f32[2,1024]{1,0:T(2,128)S(1)} %get-tuple-element.76.dep, f32[2,1024]{1,0:T(2,128)S(1)} %bitcast.25), custom_call_target="tpu_custom_call" | custom-call | bytes 1089536 | tf_op jit(solution)/shard_map/pallas_call | solution.py:33
  44.5 14.3 %collective-permute-done.8.zh = f32[44,8,128]{2,1,0:T(8,128)S(1)} collective-permute-done((f32[44,8,128]{2,1,0:T(8,128)S(1)}, f32[44,8,128]{2,1,0:T(8,128)S(1)}, u32[]{:S(2)}, u32[]{:S(2)}) %collective-permute-start.8) | collective-permute-done | bytes 180256 | tf_op jit(solution)/shard_map/ppermute | solution.py:594
  59.7 9.2 %shard_map.157 = (f32[8,64,128]{2,1,0:T(8,128)S(1)}, f32[8,64,128]{2,1,0:T(8,128)S(1)}, f32[8,64,128]{2,1,0:T(8,128)S(1)}, f32[8,64,128]{2,1,0:T(8,128)S(1)}, f3...) custom-call(s32[2]{0:T(128)S(1)} %copy-done.14, ...), custom_call_target="tpu_custom_call" | custom-call | bytes 7749640 | tf_op jit(solution)/shard_map/pallas_call | solution.py:33
  68.9 3.1 %collective-permute-start.9 = (f32[8,64,128]{2,1,0:T(8,128)S(1)}, f32[8,64,128]{2,1,0:T(8,128)S(1)}, u32[]{:S(2)}, u32[]{:S(2)}) collective-permute-start(f32[8,64,128]{2,1,0:T(8,128)S(1)} %get-tuple-element.47.f21), channel_id=1, source_target_pairs={{0,32},{32,64},{64,96},{96,128},{128,160},{160,192},{192,224},{1,3... | collective-permute-start | bytes 786440 | tf_op jit(solution)/shard_map/ppermute | solution.py:613
  72.1 1.1 %copy-done.11 = f32[200,8,128]{2,1,0:T(8,128)S(1)} copy-done((f32[200,8,128]{2,1,0:T(8,128)S(1)}, f32[200,8,128]{2,1,0:T(8,128)}, u32[]{:S(2)}) %copy-start.11) | copy-done | bytes 819224
  73.6 27.7 %all_to_all.11 = f32[256,1,128]{2,1,0:T(1,128)S(1)} all-to-all(f32[256,1,128]{2,1,0:T(1,128)S(1)} %bitcast.24), channel_id=1, replica_groups=mesh['tm'=8,'gx'=16,'gy'=2] {'tm','gx','gy'}, dimensions={0} | all-to-all | bytes 262144 | tf_op jit(solution)/shard_map/all_to_all | solution.py:620
  101.3 1.5 %shard_map.159 = (f32[2,8,64,128]{3,2,1,0:T(8,128)}, f32[2,1024]{1,0:T(2,128)S(1)}, f32[2,8,64,128]{3,2,1,0:T(8,128)}, f32[2,8,64,128]{3,2,1,0:T(8,128)}, f32[2,...) custom-call(f32[256,128]{1,0:T(8,128)S(1)} %bitcast.20, f32[2,8,64,128]{3,2,1,0:T(8,128)S(1)} %copy-done.9, ...), custom_call_target="tpu_custom_call" | custom-call | bytes 5939200 | tf_op jit(solution)/shard_map/pallas_call | solution.py:33
  (51 shorter events, 4.6 us)
Async XLA Ops:
  2.1 1.0 %copy-start = (f32[2,8,64,128]{3,2,1,0:T(8,128)S(1)}, f32[2,8,64,128]{3,2,1,0:T(8,128)}, u32[]{:S(2)}) copy-start(f32[2,8,64,128]{3,2,1,0:T(8,128)} %v.7) | copy-start | bytes 1572868
  3.1 1.0 %copy-start.2 = (f32[2,8,64,128]{3,2,1,0:T(8,128)S(1)}, f32[2,8,64,128]{3,2,1,0:T(8,128)}, u32[]{:S(2)}) copy-start(f32[2,8,64,128]{3,2,1,0:T(8,128)} %mv.7) | copy-start | bytes 1572868
  4.1 1.0 %copy-start.4 = (f32[2,8,64,128]{3,2,1,0:T(8,128)S(1)}, f32[2,8,64,128]{3,2,1,0:T(8,128)}, u32[]{:S(2)}) copy-start(f32[2,8,64,128]{3,2,1,0:T(8,128)} %we.5) | copy-start | bytes 1572868
  5.2 1.0 %copy-start.6 = (f32[2,8,64,128]{3,2,1,0:T(8,128)S(1)}, f32[2,8,64,128]{3,2,1,0:T(8,128)}, u32[]{:S(2)}) copy-start(f32[2,8,64,128]{3,2,1,0:T(8,128)} %wn.5) | copy-start | bytes 1572868
  6.2 1.0 %copy-start.8 = (f32[2,8,64,128]{3,2,1,0:T(8,128)S(1)}, f32[2,8,64,128]{3,2,1,0:T(8,128)}, u32[]{:S(2)}) copy-start(f32[2,8,64,128]{3,2,1,0:T(8,128)} %l.5) | copy-start | bytes 1572868
  7.3 1.0 %copy-start.13 = (f32[2,8,64,128]{3,2,1,0:T(8,128)S(1)}, f32[2,8,64,128]{3,2,1,0:T(8,128)}, u32[]{:S(2)}) copy-start(f32[2,8,64,128]{3,2,1,0:T(8,128)} %f.1) | copy-start | bytes 1572868
  8.3 21.9 %copy-start.1 = (f32[2,8,64,128]{3,2,1,0:T(8,128)S(1)}, f32[2,8,64,128]{3,2,1,0:T(8,128)}, u32[]{:S(2)}) copy-start(f32[2,8,64,128]{3,2,1,0:T(8,128)} %v.7) | copy-start | bytes 1572868
  8.3 21.9 %copy-start.5 = (f32[2,8,64,128]{3,2,1,0:T(8,128)S(1)}, f32[2,8,64,128]{3,2,1,0:T(8,128)}, u32[]{:S(2)}) copy-start(f32[2,8,64,128]{3,2,1,0:T(8,128)} %we.5) | copy-start | bytes 1572868
  8.3 21.9 %copy-start.7 = (f32[2,8,64,128]{3,2,1,0:T(8,128)S(1)}, f32[2,8,64,128]{3,2,1,0:T(8,128)}, u32[]{:S(2)}) copy-start(f32[2,8,64,128]{3,2,1,0:T(8,128)} %wn.5) | copy-start | bytes 1572868
  8.3 21.9 %copy-start.14 = (s32[2]{0:T(128)S(1)}, s32[2]{0:T(128)}, u32[]{:S(2)}) copy-start(s32[2]{0:T(128)} %counts.3) | copy-start | bytes 28
  9.9 20.3 %collective-permute-start.1 = (f32[86,8,128]{2,1,0:T(8,128)S(1)}, f32[86,8,128]{2,1,0:T(8,128)S(1)}, u32[]{:S(2)}, u32[]{:S(2)}) collective-permute-start(f32[86,8,128]{2,1,0:T(8,128)S(1)} %get-tuple-element.38), channel_id=1, source_target_pairs={{2,4},{3,5},{4,2},{5,3},{6,8},{7,9},{8,6},{9,7},{10,12},{11,13},{1... | collective-permute-start | bytes 1056776 | tf_op jit(solution)/shard_map/ppermute | solution.py:577
  16.1 14.1 %collective-permute-start.2 = (f32[86,8,128]{2,1,0:T(8,128)S(1)}, f32[86,8,128]{2,1,0:T(8,128)S(1)}, u32[]{:S(2)}, u32[]{:S(2)}) collective-permute-start(f32[86,8,128]{2,1,0:T(8,128)S(1)} %get-tuple-element.39), channel_id=1, source_target_pairs={{0,2},{1,3},{2,0},{3,1},{4,6},{5,7},{6,4},{7,5},{8,10},{9,11},{10,... | collective-permute-start | bytes 1056776 | tf_op jit(solution)/shard_map/ppermute | solution.py:580
  16.2 14.0 %collective-permute-start = (f32[6,64,128]{2,1,0:T(8,128)S(1)}, f32[6,64,128]{2,1,0:T(8,128)S(1)}, u32[]{:S(2)}, u32[]{:S(2)}) collective-permute-start(f32[6,64,128]{2,1,0:T(8,128)S(1)} %get-tuple-element.37.own), channel_id=1, source_target_pairs={{0,1},{1,0},{2,3},{3,2},{4,5},{5,4},{6,7},{7,6},{8,9},{9,8},{10,11... | collective-permute-start | bytes 589832 | tf_op jit(solution)/shard_map/ppermute | solution.py:578
  16.7 12.2 %collective-permute-start.4 = (f32[6,8,128]{2,1,0:T(8,128)S(1)}, f32[6,8,128]{2,1,0:T(8,128)S(1)}, u32[]{:S(2)}, u32[]{:S(2)}) collective-permute-start(f32[6,8,128]{2,1,0:T(8,128)S(1)} %slice.34), channel_id=1, source_target_pairs={{0,3},{1,2},{2,1},{3,0},{4,7},{5,6},{6,5},{7,4},{8,11},{9,10},{10,... | collective-permute-start | bytes 73736 | tf_op jit(solution)/shard_map/ppermute | solution.py:581
  18.3 11.8 %collective-permute-start.3 = (f32[6,8,128]{2,1,0:T(8,128)S(1)}, f32[6,8,128]{2,1,0:T(8,128)S(1)}, u32[]{:S(2)}, u32[]{:S(2)}) collective-permute-start(f32[6,8,128]{2,1,0:T(8,128)S(1)} %slice.33), channel_id=1, source_target_pairs={{2,5},{3,4},{4,3},{5,2},{6,9},{7,8},{8,7},{9,6},{10,13},{11,12},{1... | collective-permute-start | bytes 73736 | tf_op jit(solution)/shard_map/ppermute | solution.py:579
  28.9 29.9 %collective-permute-start.7 = (f32[200,8,128]{2,1,0:T(8,128)S(1)}, f32[200,8,128]{2,1,0:T(8,128)S(1)}, u32[]{:S(2)}, u32[]{:S(2)}) collective-permute-start(f32[200,8,128]{2,1,0:T(8,128)S(1)} %get-tuple-element.42.z_own), channel_id=1, source_target_pairs={{32,0},{64,32},{96,64},{128,96},{160,128},{192,160},{224,192},{33,... | collective-permute-start | bytes 2457608 | tf_op jit(solution)/shard_map/ppermute | solution.py:576
  30.2 11.9 %copy-start.15 = (f32[2,1,1,1024]{3,2,1,0:T(1,128)S(1)}, f32[2,1,1,1024]{3,2,1,0:T(1,128)}, u32[]{:S(2)}) copy-start(f32[2,1,1,1024]{3,2,1,0:T(1,128)} %param.17) | copy-start | bytes 24580
  36.3 23.4 %copy-start.3 = (f32[2,8,64,128]{3,2,1,0:T(8,128)S(1)}, f32[2,8,64,128]{3,2,1,0:T(8,128)}, u32[]{:S(2)}) copy-start(f32[2,8,64,128]{3,2,1,0:T(8,128)} %mv.7) | copy-start | bytes 1572868
  36.3 35.7 %collective-permute-start.5 = (f32[8,64,128]{2,1,0:T(8,128)S(1)}, f32[8,64,128]{2,1,0:T(8,128)S(1)}, u32[]{:S(2)}, u32[]{:S(2)}) collective-permute-start(f32[8,64,128]{2,1,0:T(8,128)S(1)} %get-tuple-element.40), channel_id=1, source_target_pairs={{0,32},{32,64},{64,96},{96,128},{128,160},{160,192},{192,224},{1,3... | collective-permute-start | bytes 786440 | tf_op jit(solution)/shard_map/ppermute | solution.py:606
  39.4 32.7 %collective-permute-start.6 = (f32[8,64,128]{2,1,0:T(8,128)S(1)}, f32[8,64,128]{2,1,0:T(8,128)S(1)}, u32[]{:S(2)}, u32[]{:S(2)}) collective-permute-start(f32[8,64,128]{2,1,0:T(8,128)S(1)} %get-tuple-element.41.rv0), channel_id=1, source_target_pairs={{32,0},{64,32},{96,64},{128,96},{160,128},{192,160},{224,192},{33,... | collective-permute-start | bytes 786440 | tf_op jit(solution)/shard_map/ppermute | solution.py:605
  40.8 18.0 %collective-permute-start.8 = (f32[44,8,128]{2,1,0:T(8,128)S(1)}, f32[44,8,128]{2,1,0:T(8,128)S(1)}, u32[]{:S(2)}, u32[]{:S(2)}) collective-permute-start(f32[44,8,128]{2,1,0:T(8,128)S(1)} %fusion), channel_id=1, source_target_pairs={{32,0},{64,32},{96,64},{128,96},{160,128},{192,160},{224,192},{33,... | collective-permute-start | bytes 540680 | tf_op jit(solution)/shard_map/ppermute | solution.py:594
  68.9 32.4 %collective-permute-start.9 = (f32[8,64,128]{2,1,0:T(8,128)S(1)}, f32[8,64,128]{2,1,0:T(8,128)S(1)}, u32[]{:S(2)}, u32[]{:S(2)}) collective-permute-start(f32[8,64,128]{2,1,0:T(8,128)S(1)} %get-tuple-element.47.f21), channel_id=1, source_target_pairs={{0,32},{32,64},{64,96},{96,128},{128,160},{160,192},{192,224},{1,3... | collective-permute-start | bytes 786440 | tf_op jit(solution)/shard_map/ppermute | solution.py:613
  72.1 1.1 %copy-start.11 = (f32[200,8,128]{2,1,0:T(8,128)S(1)}, f32[200,8,128]{2,1,0:T(8,128)}, u32[]{:S(2)}) copy-start(f32[200,8,128]{2,1,0:T(8,128)} %copy-done.10) | copy-start | bytes 2457604
  73.2 28.1 %copy-start.9 = (f32[2,8,64,128]{3,2,1,0:T(8,128)S(1)}, f32[2,8,64,128]{3,2,1,0:T(8,128)}, u32[]{:S(2)}) copy-start(f32[2,8,64,128]{3,2,1,0:T(8,128)} %l.5) | copy-start | bytes 1572868
  (2 other events, 1.9 us)
